TPU v7x, 32 devices: a whole 2x2x4 slice. The times are simulated.
32 devices in a mesh: dp: 16 (over z, x, core), blk: 2 (over y).
Axes of the slice: x: 2, y: 2, z: 4, core: 2. Of those that a mesh axis runs over, the one named last changes fastest.
Arguments:
- tokens: bfloat16 [16, 1280, 768], P('dp', 'blk'), may hold values from -6 to 6
- segment_ids: int32 [16, 1280], P('dp', 'blk'), may hold values from 0 to 6, as said below
- gain_attn: float32 [768], replicated, may hold values from 0.5 to 1.5
- w_qkv: bfloat16 [768, 2304], replicated, may hold values from -0.21875 to 0.21875
- w_out: bfloat16 [768, 768], replicated, may hold values from -2.5 to 2.5
- gain_ffn: float32 [768], replicated, may hold values from 0.5 to 1.5
- w_up: bfloat16 [768, 3072], replicated, may hold values from -0.21875 to 0.21875
- w_down: bfloat16 [3072, 768], replicated, may hold values from -0.109375 to 0.109375
- cotangent: bfloat16 [16, 1280, 768], P('dp', 'blk'), may hold values from -6 to 6
Outputs:
- layer_out: float32 [16, 1280, 768], P('dp', 'blk')
- input_grad: float32 [16, 1280, 768], P('dp', 'blk')
- grad_gain_attn: float32 [768], P('dp')
- grad_qkv: float32 [768, 2304], P('dp', 'blk')
- grad_out: float32 [768, 768], P('dp', 'blk')
- grad_gain_ffn: float32 [768], P('dp')
- grad_up: float32 [768, 3072], P('dp', 'blk')
- grad_down: float32 [3072, 768], P('dp', 'blk')
Inputs may be any that keep to these rules, and one draw needn't show every extreme that they name: Each sequence is packed with whole images of 197 or 577 positions, the last one cut at the sequence's end; segment_ids start at 0 and rise by one at each new image; one sequence holds only images of 197 positions.
All inputs are finite; a program needn't handle non-finite values.
Results may differ from a plain program's by a relative error of at most 0.02.
Values may be sent and summed in bfloat16 or wider, within the bound.
A program may use at most 192 MiB of HBM per device.

v0:
```python
from functools import partial
import math

import jax
import jax.numpy as jnp
from jax import lax
from jax.sharding import PartitionSpec as P

HEADS = 12


def padded(block, sides, width):
    for axis, dim in sides:
        count = lax.axis_size(axis)
        forward = [(i, i + 1) for i in range(count - 1)]
        backward = [(target, source) for source, target in forward]
        low = lax.ppermute(
            lax.slice_in_dim(block, block.shape[dim] - width, None, axis=dim), axis, forward
        )
        high = lax.ppermute(lax.slice_in_dim(block, 0, width, axis=dim), axis, backward)
        block = jnp.concatenate([low, block, high], axis=dim)
    return block


def from_behind(block, axis, distance):
    devices = range(lax.axis_size(axis))
    route = [(i - distance, i) for i in devices if i - distance in devices]
    return lax.ppermute(block, axis, route)


def normalize(values):
    centered = values - jnp.mean(values, -1, keepdims=True)
    variance = jnp.mean(centered * centered, -1, keepdims=True)
    inverse = lax.rsqrt(variance + 1e-05)
    return (centered * inverse, inverse)


def norm_back(grad_normed, normed, inverse):
    first = jnp.mean(grad_normed, -1, keepdims=True)
    second = jnp.mean(grad_normed * normed, -1, keepdims=True)
    return inverse * (grad_normed - first - normed * second)


def split_blocks(packed, seg_all):
    length = packed.shape[0]
    feature_count = packed.shape[1] // 2
    block_rows = math.gcd(length, 512)
    count_blocks = length // block_rows
    keys_blk = packed[:, :feature_count].reshape(
        count_blocks, block_rows, HEADS, feature_count // HEADS
    )
    vals_blk = packed[:, feature_count:].reshape(
        count_blocks, block_rows, HEADS, feature_count // HEADS
    )
    seg_blk = seg_all.reshape(count_blocks, block_rows)
    return (keys_blk, vals_blk, seg_blk)


def fetch_near(kv_local, seg_mark):
    return (
        padded(kv_local, (("blk", 0),), kv_local.shape[0]),
        padded(seg_mark, (("blk", 0),), kv_local.shape[0]),
    )


def block_scores(query_rows, keys_rows, seg_query, seg_keys):
    scale_factor = query_rows.shape[-1] ** (-0.5)
    scores = (
        jnp.einsum("qhd,khd->hqk", query_rows, keys_rows, preferred_element_type=jnp.float32)
        * scale_factor
    )
    allowed = (seg_query[:, None] == seg_keys[None, :])[None]
    return (jnp.where(allowed, scores, -1e30), allowed)


def attend_forward(query_rows, keys_blk, vals_blk, seg_blk, seg_query):
    row_count = query_rows.shape[0]

    def stats_step(carried, block_item):
        running, totals = carried
        scores, allowed = block_scores(query_rows, block_item[0], seg_query, block_item[1])
        newest = jnp.maximum(running, jnp.max(scores, -1))
        fresh = jnp.sum(jnp.where(allowed, jnp.exp(scores - newest[..., None]), 0.0), -1)
        return ((newest, totals * jnp.exp(running - newest) + fresh), None)

    start_max = jnp.full((HEADS, row_count), -1e30, jnp.float32)
    start_tot = jnp.zeros((HEADS, row_count), jnp.float32)
    (running, totals), unused = lax.scan(stats_step, (start_max, start_tot), (keys_blk, seg_blk))
    logsum = running + jnp.log(totals)

    def value_step(carried, block_item):
        scores, allowed = block_scores(query_rows, block_item[0], seg_query, block_item[2])
        prob_rows = jnp.where(allowed, jnp.exp(scores - logsum[..., None]), 0.0).astype(
            jnp.bfloat16
        )
        return (
            carried
            + jnp.einsum(
                "hqk,khd->qhd", prob_rows, block_item[1], preferred_element_type=jnp.float32
            ),
            None,
        )

    start_mix = jnp.zeros(query_rows.shape, jnp.float32)
    mixed, unused_two = lax.scan(value_step, start_mix, (keys_blk, vals_blk, seg_blk))
    return (mixed, logsum)


def attend_backward(
    query_rows, keys_blk, vals_blk, seg_blk, seg_query, logsum, grad_mixed, delta_rows
):
    scale_factor = query_rows.shape[-1] ** (-0.5)

    def grad_step(carried, block_item):
        keys_rows, vals_rows, seg_keys = block_item
        scores, allowed = block_scores(query_rows, keys_rows, seg_query, seg_keys)
        prob_rows = jnp.where(allowed, jnp.exp(scores - logsum[..., None]), 0.0)
        grad_vals = jnp.einsum(
            "hqk,qhd->khd",
            prob_rows.astype(jnp.bfloat16),
            grad_mixed,
            preferred_element_type=jnp.float32,
        )
        grad_probs = jnp.einsum(
            "qhd,khd->hqk", grad_mixed, vals_rows, preferred_element_type=jnp.float32
        )
        grad_scores = (prob_rows * (grad_probs - delta_rows[..., None])).astype(jnp.bfloat16)
        carried = (
            carried
            + jnp.einsum("hqk,khd->qhd", grad_scores, keys_rows, preferred_element_type=jnp.float32)
            * scale_factor
        )
        grad_keys = (
            jnp.einsum("hqk,qhd->khd", grad_scores, query_rows, preferred_element_type=jnp.float32)
            * scale_factor
        )
        return (carried, (grad_keys, grad_vals))

    start_grad = jnp.zeros(query_rows.shape, jnp.float32)
    grad_query, (grad_keys, grad_vals) = lax.scan(
        grad_step, start_grad, (keys_blk, vals_blk, seg_blk)
    )
    return (grad_query, grad_keys, grad_vals)


def per_device(tokens, segment_ids, gain_attn, w_qkv, w_out, gain_ffn, w_up, w_down, cotangent):
    inputs = tokens[0].astype(jnp.float32)
    seg_mark = segment_ids[0] + 1
    row_count, feature_count = inputs.shape
    head_size = feature_count // HEADS
    normed_one, inverse_one = normalize(inputs)
    attn_in = (normed_one * gain_attn).astype(jnp.bfloat16)
    projected = jnp.dot(attn_in, w_qkv, preferred_element_type=jnp.float32).astype(jnp.bfloat16)
    query_rows = projected[:, :feature_count].reshape(row_count, HEADS, head_size)
    kv_local = projected[:, feature_count:]
    packed, seg_near = fetch_near(kv_local, seg_mark)
    keys_blk, vals_blk, seg_blk = split_blocks(packed, seg_near)
    mixed, logsum = attend_forward(query_rows, keys_blk, vals_blk, seg_blk, seg_mark)
    mixed_b = mixed.reshape(row_count, feature_count).astype(jnp.bfloat16)
    middle = inputs + jnp.dot(mixed_b, w_out, preferred_element_type=jnp.float32)
    normed_two, inverse_two = normalize(middle)
    ffn_in = (normed_two * gain_ffn).astype(jnp.bfloat16)
    hidden = jnp.dot(ffn_in, w_up, preferred_element_type=jnp.float32)
    active, gelu_back = jax.vjp(partial(jax.nn.gelu, approximate=False), hidden)
    active_b = active.astype(jnp.bfloat16)
    layer_out = middle + jnp.dot(active_b, w_down, preferred_element_type=jnp.float32)
    upstream_b = cotangent[0]
    upstream = upstream_b.astype(jnp.float32)
    grad_down = jnp.einsum("nf,nd->fd", active_b, upstream_b, preferred_element_type=jnp.float32)
    grad_active = jnp.einsum("nd,fd->nf", upstream_b, w_down, preferred_element_type=jnp.float32)
    grad_hidden = gelu_back(grad_active)[0].astype(jnp.bfloat16)
    grad_up = jnp.einsum("nd,nf->df", ffn_in, grad_hidden, preferred_element_type=jnp.float32)
    grad_ffn_in = jnp.einsum("nf,df->nd", grad_hidden, w_up, preferred_element_type=jnp.float32)
    grad_gain_ffn = jnp.sum(grad_ffn_in * normed_two, 0)
    grad_middle = upstream + norm_back(grad_ffn_in * gain_ffn, normed_two, inverse_two)
    grad_branch = grad_middle.astype(jnp.bfloat16)
    grad_out = jnp.einsum("nd,ne->de", mixed_b, grad_branch, preferred_element_type=jnp.float32)
    grad_mixed = jnp.einsum(
        "ne,de->nd", grad_branch, w_out, preferred_element_type=jnp.float32
    ).astype(jnp.bfloat16)
    grad_mixed = grad_mixed.reshape(row_count, HEADS, head_size)
    delta_rows = jnp.einsum("qhd,qhd->hq", grad_mixed.astype(jnp.float32), mixed)
    grad_query, grad_keys, grad_vals = attend_backward(
        query_rows, keys_blk, vals_blk, seg_blk, seg_mark, logsum, grad_mixed, delta_rows
    )
    near_rows = 3 * row_count
    kv_terms = jnp.concatenate(
        [grad_keys.reshape(near_rows, feature_count), grad_vals.reshape(near_rows, feature_count)],
        1,
    )
    lower_rim = kv_terms[:row_count]
    own_rows = kv_terms[row_count : 2 * row_count]
    upper_rim = kv_terms[2 * row_count :]
    from_right = from_behind(lower_rim.astype(jnp.bfloat16), "blk", -1).astype(lower_rim.dtype)
    from_left = from_behind(upper_rim.astype(jnp.bfloat16), "blk", 1).astype(upper_rim.dtype)
    kv_home = own_rows + from_right + from_left
    grad_proj = jnp.concatenate([grad_query.reshape(row_count, feature_count), kv_home], 1).astype(
        jnp.bfloat16
    )
    grad_qkv = jnp.einsum("nd,ne->de", attn_in, grad_proj, preferred_element_type=jnp.float32)
    grad_attn_in = jnp.einsum("ne,de->nd", grad_proj, w_qkv, preferred_element_type=jnp.float32)
    grad_gain_attn = jnp.sum(grad_attn_in * normed_one, 0)
    input_grad = grad_middle + norm_back(grad_attn_in * gain_attn, normed_one, inverse_one)
    part_qkv, part_out, part_up, part_down, part_gain_attn, part_gain_ffn = (
        lax.psum_scatter(
            grad_qkv.astype(jnp.bfloat16), "dp", scatter_dimension=0, tiled=True
        ).astype(jnp.float32),
        lax.psum_scatter(
            grad_out.astype(jnp.bfloat16), "dp", scatter_dimension=0, tiled=True
        ).astype(jnp.float32),
        lax.psum_scatter(
            grad_up.astype(jnp.bfloat16), "dp", scatter_dimension=0, tiled=True
        ).astype(jnp.float32),
        lax.psum_scatter(
            grad_down.astype(jnp.bfloat16), "dp", scatter_dimension=0, tiled=True
        ).astype(jnp.float32),
        lax.psum_scatter(
            grad_gain_attn.astype(jnp.bfloat16), "dp", scatter_dimension=0, tiled=True
        ).astype(jnp.float32),
        lax.psum_scatter(
            grad_gain_ffn.astype(jnp.bfloat16), "dp", scatter_dimension=0, tiled=True
        ).astype(jnp.float32),
    )
    sum_qkv, sum_out, sum_up, sum_down = (
        lax.psum_scatter(
            part_qkv.astype(jnp.bfloat16), "blk", scatter_dimension=1, tiled=True
        ).astype(jnp.float32),
        lax.psum_scatter(
            part_out.astype(jnp.bfloat16), "blk", scatter_dimension=1, tiled=True
        ).astype(jnp.float32),
        lax.psum_scatter(
            part_up.astype(jnp.bfloat16), "blk", scatter_dimension=1, tiled=True
        ).astype(jnp.float32),
        lax.psum_scatter(
            part_down.astype(jnp.bfloat16), "blk", scatter_dimension=1, tiled=True
        ).astype(jnp.float32),
    )
    total_gain_attn, total_gain_ffn = lax.psum((part_gain_attn, part_gain_ffn), "blk")
    return (
        layer_out[None],
        input_grad[None],
        total_gain_attn,
        sum_qkv,
        sum_out,
        total_gain_ffn,
        sum_up,
        sum_down,
    )


def solution(mesh):
    return jax.shard_map(
        per_device,
        mesh=mesh,
        in_specs=(
            P("dp", "blk", None),
            P("dp", "blk"),
            P(),
            P(),
            P(),
            P(),
            P(),
            P(),
            P("dp", "blk", None),
        ),
        out_specs=(
            P("dp", "blk", None),
            P("dp", "blk", None),
            P("dp"),
            P("dp", "blk"),
            P("dp", "blk"),
            P("dp"),
            P("dp", "blk"),
            P("dp", "blk"),
        ),
        check_vma=False,
    )
```

profile of v0, /device:TPU:0, one launch (start us, length us, event | category | flops | bytes accessed | tf_op | source)
XLA Modules:
  0.0 1232.0 jit_solution(6543701009149608048)
XLA Ops:
  33.8 29.2 %collective-permute-done.2 = s32[640]{0:T(1024)S(1)} collective-permute-done((s32[640]{0:T(1024)S(1)}, s32[640]{0:T(1024)S(1)}, u32[]{:S(2)}, u32[]{:S(2)}) %collective-permute-start.2) | collective-permute-done | bytes 2592 | tf_op jit(solution)/shard_map/ppermute | solution.py:17
  90.8 158.8 %while.39 = (s32[]{:T(128)}, f32[12,640]{1,0:T(8,128)}, f32[12,640]{1,0:T(8,128)}, s32[640]{0:T(1024)S(1)}, s32[15,128]{1,0:T(8,128)S(1)}, /*index=5*/bf16[15,12...) while((s32[]{:T(128)}, f32[12,640]{1,0:T(8,128)}, ...), condition=%wide.region_5.6_spmd.clone, body=%wide.region_2.5_spmd.clone.sunk | while | flops 133813760 | bytes 10390236 | solution.py:88
  265.2 85.9 %while.40 = (s32[]{:T(128)}, f32[640,12,64]{0,2,1:T(8,128)}, bf16[15,128,12,64]{1,3,2,0:T(8,128)(2,1)}, s32[640]{0:T(1024)S(1)}, s32[15,128]{1,0:T(8,128)S(1)}, ...) while((s32[]{:T(128)}, f32[640,12,64]{0,2,1:T(8,128)}, ...), condition=%wide.region_7.8_spmd.clone, body=%wide.region_6.7_spmd.clone.sunk | while | flops 257638400 | bytes 5518451 | solution.py:105
  356.2 24.5 %multiply_convert_fusion = (bf16[640,3072]{1,0:T(8,128)(2,1)}, f32[640,3072]{1,0:T(8,128)}, f32[640,3072]{1,0:T(8,128)}) fusion(bf16[768,3072]{1,0:T(8,128)(2,1)S(1)} %bitcast.260, f32[640,768]{1,0:T(8,128)S(1)} %get-tuple-element.402, f32[768]{0:T(1024)S(1)} %copy-done.26, f32[640]{0:T(1024)S(1)} %add_rsqrt_fusion, f32[640]{0:T(1024)S(1)} %broadcast_multiply_fusion.4), kind=kOutput, calls=%fused_computation.60 | convolution fusion | flops 3149660160 | bytes 26353664 | tf_op jit(solution)/shard_map/dot_general | solution.py:163
  431.4 24.6 %reduce-scatter.17.cloned.1.call-done = bf16[48,768]{1,0:T(8,128)(2,1)} async-done(((bf16[768,768]{1,0:T(8,128)(2,1)}), bf16[48,768]{1,0:T(8,128)(2,1)}) %reduce-scatter.17.cloned.1.call-update) | async-done | bytes 73744 | tf_op jit(solution)/shard_map/reduce_scatter | solution.py:208
  460.6 570.1 %while.41 = (s32[]{:T(128)}, f32[640,12,64]{0,2,1:T(8,128)}, f32[15,128,12,64]{1,0,3,2:T(8,128)}, f32[15,128,12,64]{1,0,3,2:T(8,128)}, bf16[15,128,12,64]{1,3,2,...) while((s32[]{:T(128)}, f32[640,12,64]{0,2,1:T(8,128)}, ...), condition=%wide.region_13.14_spmd.clone, body=%wide.region_12.13_spmd.clone.sunk | while | flops 642596864 | bytes 60882780 | solution.py:140
  468.2 11.1 dynamic_update_slice.11
  483.8 11.1 dynamic_update_slice.12
  521.2 11.1 dynamic_update_slice.12
  559.3 11.2 dynamic_update_slice.12
  597.6 11.1 dynamic_update_slice.12
  635.6 11.0 dynamic_update_slice.12
  673.6 11.0 dynamic_update_slice.12
  711.5 11.0 dynamic_update_slice.12
  749.5 11.0 dynamic_update_slice.12
  772.0 11.1 dynamic_update_slice.11
  787.5 11.0 dynamic_update_slice.12
  810.0 11.1 dynamic_update_slice.11
  825.5 11.0 dynamic_update_slice.12
  848.0 11.1 dynamic_update_slice.11
  863.5 11.0 dynamic_update_slice.12
  886.0 11.1 dynamic_update_slice.11
  924.0 11.1 dynamic_update_slice.11
  939.5 11.0 dynamic_update_slice.12
  962.0 11.1 dynamic_update_slice.11
  1000.0 11.1 dynamic_update_slice.11
  1015.5 11.0 dynamic_update_slice.12
  1056.2 38.4 %collective-permute-done.4 = bf16[640,1536]{0,1:T(8,128)(2,1)S(1)} collective-permute-done((bf16[640,1536]{0,1:T(8,128)(2,1)S(1)}, bf16[640,1536]{0,1:T(8,128)(2,1)S(1)}, u32[]{:S(2)}, u32[]{:S(2)}) %collective-permute-start.4) | collective-permute-done | bytes 1966112 | tf_op jit(solution)/shard_map/ppermute | solution.py:28
  1128.5 30.6 %all-reduce.3 = (bf16[768]{0:T(1024)(128)(2,1)}, bf16[768]{0:T(1024)(128)(2,1)S(1)}) all-reduce(bf16[768]{0:T(1024)(128)(2,1)} %get-tuple-element.331, bf16[768]{0:T(1024)(128)(2,1)} %get-tuple-element.329), channel_id=2, replica_groups=mesh['dp'=16,'blk'=2] {'dp'}, use_global_device_ids=true, to_apply=%region_17.18.clone | all-reduce | flops 1536 | bytes 6144
  1160.3 14.9 %reduce-scatter.15.cloned.1.call-done = bf16[48,2304]{1,0:T(8,128)(2,1)} async-done(((bf16[768,2304]{1,0:T(8,128)(2,1)}), bf16[48,2304]{1,0:T(8,128)(2,1)}) %reduce-scatter.15.cloned.1.call-update) | async-done | bytes 221200 | tf_op jit(solution)/shard_map/reduce_scatter | solution.py:205
  1192.7 11.1 reduce-scatter.21.cloned.1.call-done
  1205.4 16.0 %reduce-scatter.25.cloned.1.call-done = bf16[1152,48]{1,0:T(8,128)(2,1)} async-done(((bf16[2304,48]{1,0:T(8,128)(2,1)}), bf16[1152,48]{1,0:T(8,128)(2,1)}) %reduce-scatter.25.cloned.1.call-update) | async-done | bytes 110608
  (747 shorter events, 792.0 us)
Async XLA Ops:
  7.2 448.8 %reduce-scatter.17.cloned.1.call-start = ((), (), s32[]{:S(2)}) async-start(), calls=%async_computation.9 | async-start | bytes 1253376 | tf_op jit(solution)/shard_map/reduce_scatter | solution.py:208
  8.8 5.5 copy-start.21
  14.3 8.8 copy-start.29
  15.7 53.9 %collective-permute-start = (bf16[640,1536]{1,0:T(8,128)(2,1)}, bf16[640,1536]{1,0:T(8,128)(2,1)}, u32[]{:S(2)}, u32[]{:S(2)}) collective-permute-start(bf16[640,1536]{1,0:T(8,128)(2,1)} %slice.30), channel_id=1, source_target_pairs={{0,1},{2,3},{4,5},{6,7},{8,9},{10,11},{12,13},{14,15},{16,17},{18,... | collective-permute-start | bytes 5898248 | tf_op jit(solution)/shard_map/ppermute | solution.py:17
  21.8 47.8 %collective-permute-start.1 = (bf16[640,1536]{1,0:T(8,128)(2,1)}, bf16[640,1536]{1,0:T(8,128)(2,1)}, u32[]{:S(2)}, u32[]{:S(2)}) collective-permute-start(bf16[640,1536]{1,0:T(8,128)(2,1)} %slice.30), channel_id=1, source_target_pairs={{1,0},{3,2},{5,4},{7,6},{9,8},{11,10},{13,12},{15,14},{17,16},{19,... | collective-permute-start | bytes 5898248 | tf_op jit(solution)/shard_map/ppermute | solution.py:20
  23.1 39.8 %collective-permute-start.2 = (s32[640]{0:T(1024)S(1)}, s32[640]{0:T(1024)S(1)}, u32[]{:S(2)}, u32[]{:S(2)}) collective-permute-start(s32[640]{0:T(1024)S(1)} %add_reduce_fusion), channel_id=1, source_target_pairs={{0,1},{2,3},{4,5},{6,7},{8,9},{10,11},{12,13},{14,15},{16,17},{18,... | collective-permute-start | bytes 7688 | tf_op jit(solution)/shard_map/ppermute | solution.py:17
  29.0 39.4 %collective-permute-start.3 = (s32[640]{0:T(1024)S(1)}, s32[640]{0:T(1024)S(1)}, u32[]{:S(2)}, u32[]{:S(2)}) collective-permute-start(s32[640]{0:T(1024)S(1)} %add_reduce_fusion), channel_id=1, source_target_pairs={{1,0},{3,2},{5,4},{7,6},{9,8},{11,10},{13,12},{15,14},{17,16},{19,... | collective-permute-start | bytes 7688 | tf_op jit(solution)/shard_map/ppermute | solution.py:20
  260.2 4.3 copy-start.16
  351.1 4.6 copy-start.25
  351.1 5.0 slice-start.2
  352.9 27.7 %slice-start.4 = ((s8[4718592]{0:T(1024)(128)(4,1)}), s8[4194304]{0:T(1024)(128)(4,1)S(1)}, s32[]{:S(2)}) async-start(s8[4718592]{0:T(1024)(128)(4,1)} %bitcast.261), calls=%async_computation.20 | async-start | bytes 8388608
  355.7 37.7 %copy-start.8 = (f32[640,768]{1,0:T(8,128)}, f32[640,768]{1,0:T(8,128)S(1)}, u32[]{:S(2)}) copy-start(f32[640,768]{1,0:T(8,128)S(1)} %get-tuple-element.402) | copy-start | bytes 5898244
  356.1 24.5 %copy-start.17 = (bf16[1,640,768]{2,1,0:T(8,128)(2,1)S(1)}, bf16[1,640,768]{2,1,0:T(8,128)(2,1)}, u32[]{:S(2)}) copy-start(bf16[1,640,768]{2,1,0:T(8,128)(2,1)} %param.23) | copy-start | bytes 2949124
  356.2 24.5 %slice-start.5 = ((s8[4718592]{0:T(1024)(128)(4,1)}), s8[524288]{0:T(1024)(128)(4,1)S(1)}, s32[]{:S(2)}) async-start(s8[4718592]{0:T(1024)(128)(4,1)} %bitcast.261), calls=%async_computation.21 | async-start | bytes 1048576
  397.5 709.9 %reduce-scatter.23.cloned.1.call-start = ((), (), s32[]{:S(2)}) async-start(), calls=%async_computation.12 | async-start | bytes 5013504 | tf_op jit(solution)/shard_map/reduce_scatter | solution.py:214
  416.4 702.1 %reduce-scatter.27.cloned.1.call-start = ((), (), s32[]{:S(2)}) async-start(), calls=%async_computation.14 | async-start | bytes 294912
  457.7 663.7 %reduce-scatter.19.cloned.1.call-start = ((), (), s32[]{:S(2)}) async-start(), calls=%async_computation.10 | async-start | bytes 5013504 | tf_op jit(solution)/shard_map/reduce_scatter | solution.py:211
  460.6 714.6 %reduce-scatter.15.cloned.1.call-start = ((), (), s32[]{:S(2)}) async-start(), calls=%async_computation.8 | async-start | bytes 3760128 | tf_op jit(solution)/shard_map/reduce_scatter | solution.py:205
  1030.7 8.4 slice-start
  1030.7 8.4 slice-start.1
  1049.4 6.6 copy-start.4
  1049.8 44.9 %collective-permute-start.4 = (bf16[640,1536]{0,1:T(8,128)(2,1)S(1)}, bf16[640,1536]{0,1:T(8,128)(2,1)S(1)}, u32[]{:S(2)}, u32[]{:S(2)}) collective-permute-start(bf16[640,1536]{0,1:T(8,128)(2,1)S(1)} %get-tuple-element.397), channel_id=1, source_target_pairs={{1,0},{3,2},{5,4},{7,6},{9,8},{11,10},{13,12},{15,14},{17,16},{19,... | collective-permute-start | bytes 5898248 | tf_op jit(solution)/shard_map/ppermute | solution.py:28
  1051.2 44.7 %collective-permute-start.5 = (bf16[640,1536]{0,1:T(8,128)(2,1)S(1)}, bf16[640,1536]{0,1:T(8,128)(2,1)S(1)}, u32[]{:S(2)}, u32[]{:S(2)}) collective-permute-start(bf16[640,1536]{0,1:T(8,128)(2,1)S(1)} %get-tuple-element.398), channel_id=1, source_target_pairs={{0,1},{2,3},{4,5},{6,7},{8,9},{10,11},{12,13},{14,15},{16,17},{18,... | collective-permute-start | bytes 5898248 | tf_op jit(solution)/shard_map/ppermute | solution.py:28
  1056.1 42.7 %copy-start.18 = (bf16[640,12,64]{0,2,1:T(8,128)(2,1)}, bf16[640,12,64]{0,2,1:T(8,128)(2,1)S(1)}, u32[]{:S(2)}) copy-start(bf16[640,12,64]{0,2,1:T(8,128)(2,1)S(1)} %convert.11) | copy-start | bytes 2949124
  1056.2 43.9 %copy-start.6 = (bf16[1,640,768]{2,1,0:T(8,128)(2,1)S(1)}, bf16[1,640,768]{2,1,0:T(8,128)(2,1)}, u32[]{:S(2)}) copy-start(bf16[1,640,768]{2,1,0:T(8,128)(2,1)} %param.15) | copy-start | bytes 2949124
  1056.2 43.9 %copy-start.22 = (f32[640]{0:T(1024)S(1)}, f32[640]{0:T(1024)}, u32[]{:S(2)}) copy-start(f32[640]{0:T(1024)} %copy-done.21) | copy-start | bytes 7684
  1056.2 43.9 %copy-start.24 = (f32[640]{0:T(1024)S(1)}, f32[640]{0:T(1024)}, u32[]{:S(2)}) copy-start(f32[640]{0:T(1024)} %copy-done.23) | copy-start | bytes 7684
  1056.2 43.9 %copy-start.27 = (f32[768]{0:T(1024)S(1)}, f32[768]{0:T(1024)}, u32[]{:S(2)}) copy-start(f32[768]{0:T(1024)} %param.17) | copy-start | bytes 9220
  1100.1 6.1 copy-start.30
  1106.2 83.2 %reduce-scatter.29.cloned.1.call-start = ((), (), s32[]{:S(2)}) async-start(), calls=%async_computation.15 | async-start | bytes 589824
  1109.4 94.3 %reduce-scatter.21.cloned.1.call-start = ((), (), s32[]{:S(2)}) async-start(), calls=%async_computation.11 | async-start | bytes 442368 | tf_op jit(solution)/shard_map/reduce_scatter | solution.py:231
  1121.5 99.9 %reduce-scatter.25.cloned.1.call-start = ((), (), s32[]{:S(2)}) async-start(), calls=%async_computation.13 | async-start | bytes 884736
  (174 other events, 461.4 us)
Sparse Core Ops, SparseCore 0:
  397.6 58.3 reduce-scatter.16
  459.9 74.6 reduce-scatter.22
  537.5 9.9 reduce-scatter.26
  551.7 75.5 reduce-scatter.18
  1106.3 68.8 reduce-scatter.14
  1177.3 11.9 reduce-scatter.28
  1191.6 12.0 reduce-scatter.20
  1206.1 15.2 reduce-scatter.24
where the time goes:
time: 1250 us; the launch traced here: 1230 us
  matrix products  456 us (36%)
  local copies, waits for them, and re-layouts  439 us (35%)
  waiting for transfers between devices  142 us (11%)
  other arithmetic  109 us (9%)
  blocking collectives  36.1 us (3%)
  starting transfers between devices  31.8 us (3%)
  between operations  15.7 us (1%)
    dynamic_update_slice x30, local copies, waits for them, and re-layouts, attend_backward(): lax.scan(grad_step, start_grad, (keys_blk, vals_blk, seg_blk))  331 us
    dot_general x30, matrix products, block_scores(): jnp.einsum('qhd,khd->hqk', query_rows, keys_rows, preferred_element_type=...  100 us
    dot_general x15, matrix products, value_step(): jnp.einsum('hqk,khd->qhd', prob_rows, block_item[1], preferred_element_ty...  74.5 us
    dot_general x15, matrix products, grad_step(): jnp.einsum('hqk,qhd->khd', prob_rows.astype(jnp.bfloat16), grad_mixed, pr...  66.4 us
    dot_general x15, matrix products, grad_step(): jnp.einsum('hqk,khd->qhd', grad_scores, keys_rows, preferred_element_type...  59.7 us
    reduce_sum x15, other arithmetic, stats_step(): jnp.sum(jnp.where(allowed, jnp.exp(scores - newest[..., None]), 0.0), -1)  46.4 us
    dot_general x15, matrix products, grad_step(): jnp.einsum('qhd,khd->hqk', grad_mixed, vals_rows, preferred_element_type=...  42 us
    ppermute x2, waiting for transfers between devices, from_behind(): return lax.ppermute(block, axis, route)  39.7 us
  transfers between devices with their start and end apart: 14, of which 9 were waited for; matrix products, arithmetic and copies ran while one was open for 54% of the time, Pallas kernels for 0%

commit v1 on v0

--- a/solution.py
+++ b/solution.py
@@ -1,12 +1,1050 @@
 from functools import partial
 import math
+from types import SimpleNamespace
 
 import jax
 import jax.numpy as jnp
 from jax import lax
+from jax.experimental import pallas as pl
+from jax.experimental.pallas import tpu as pltpu
 from jax.sharding import PartitionSpec as P
 
 HEADS = 12
+NEG = -1e30
+LOG2E = math.log2(math.e)
+IMAGES = (197, 577)
+REACH = 576
+TILE = 128
+UNIT = 128
+F32, BF16 = jnp.float32, jnp.bfloat16
+MESH = pl.DeviceIdType.MESH
+NN = (((1,), (0,)), ((), ()))
+NT = (((1,), (1,)), ((), ()))
+BITS = ("core", "x", "z0", "z1", "y")
+ORDER_A = ("core", "x", "y", "z0", "z1")
+ORDER_B = ("core", "z0", "z1", "x", "y")
+ORDER_C = ("core", "y", "x", "z0", "z1")
+ORDER_D = ("core", "z0", "z1", "y", "x")
+ORDER_E = ("core", "x", "z0", "z1", "y")
+OUT_AFTER = 5
+ORDERS = (ORDER_C, ORDER_E, ORDER_C, ORDER_E, ORDER_C, ORDER_E, ORDER_A, ORDER_E, ORDER_D, ORDER_C, ORDER_C, ORDER_D, ORDER_A, ORDER_D, ORDER_A, ORDER_D, ORDER_A)
+ENDS = {
+    ("ff", 2): ((0, 0), (1, 0),),
+    ("ff", 4): ((0, 1), (2, 0), (3, 0),),
+    ("dn", 1): ((2, 1),),
+    ("dn", 2): ((3, 1), (4, 0), (5, 0),),
+    ("gm", 0): ((0, 2), (1, 1),),
+    ("de", 0): ((2, 2),),
+    ("own", 0): ((0, 3), (2, 3), (1, 2), (3, 2), (4, 1), (5, 1), (6, 0),),
+    ("own", 1): ((8, 0),),
+    ("own", 2): ((0, 4), (2, 4), (1, 3), (3, 3), (4, 2), (5, 2), (7, 0),),
+    ("own", 3): ((1, 4), (3, 4), (4, 3), (5, 3), (6, 1),),
+    ("own", 4): ((4, 4), (5, 4), (8, 1),),
+    ("out", 0): ((7, 1),),
+    ("own", 5): ((6, 2), (9, 0),),
+    ("oth", 2): ((7, 2), (8, 2),),
+    ("oth", 3): ((6, 3), (9, 1),),
+    ("oth", 4): ((8, 3), (10, 0), (11, 0), (12, 0),),
+    ("oth", 5): ((6, 4), (7, 3), (9, 2), (13, 0), (14, 0),),
+    ("tail", 0): ((8, 4), (11, 1), (12, 1), (15, 0), (16, 0),),
+    ("tail", 1): ((7, 4), (9, 3), (14, 1),),
+    ("tail", 2): ((13, 1),),
+    ("tail", 4): ((12, 2), (10, 1),),
+    ("tail", 5): ((16, 1),),
+    ("tail", 6): ((11, 2),),
+    ("tail", 7): ((14, 2), (9, 4), (11, 3), (12, 3), (16, 2), (15, 1), (14, 3), (10, 2), (13, 2), (11, 4), (12, 4), (16, 3), (13, 3), (14, 4), (13, 4), (16, 4), (15, 2), (10, 3), (15, 3), (10, 4), (15, 4),),
+}
+
+
+def dot(a, b, dims=NN):
+    return lax.dot_general(a, b, dims, preferred_element_type=F32)
+
+
+def aligned(value, unit):
+    return pl.multiple_of(value, unit)
+
+
+def tile_at(index):
+    return pl.ds(aligned(index * TILE, TILE), TILE)
+
+
+def chunks(total, size):
+    return [(at, min(size, total - at)) for at in range(0, total, size)]
+
+
+def interleave(first, second):
+    first, second = list(first), list(second)
+    done = 0
+    for k, step in enumerate(first):
+        step()
+        upto = (k + 1) * len(second) // len(first)
+        for other in second[done:upto]:
+            other()
+        done = upto
+    for other in second[done:]:
+        other()
+
+
+def pipeline(before, during, after):
+    count = len(during)
+    for step in before[0]:
+        step()
+    for n in range(count):
+        matrix = (list(after[n - 1]) if n else []) + (list(before[n + 1]) if n + 1 < count else [])
+        interleave(matrix, during[n])
+    for step in after[count - 1]:
+        step()
+
+
+def pair_rows(slab):
+    first = lax.broadcasted_iota(jnp.int32, slab.shape, 1) < slab.shape[1] // 2
+    zero = jnp.zeros_like(slab)
+    return jnp.concatenate([jnp.where(first, slab, zero), jnp.where(first, zero, slab)], 0)
+
+
+def own_halves(block):
+    half = TILE // 2
+    return jnp.concatenate([block[:half, :TILE], block[half:TILE, TILE:]], 0)
+
+
+def fold_sum(block):
+    return jnp.sum(block.reshape(block.shape[0] // 8, 8, block.shape[1]), 0)
+
+
+def standardize(values):
+    mean = jnp.mean(values, -1, keepdims=True)
+    centered = values - mean
+    variance = jnp.mean(centered * centered, -1, keepdims=True)
+    inverse = lax.rsqrt(variance + 1e-05)
+    return centered * inverse, inverse
+
+
+def norm_backward(grad, normed, inverse):
+    first = jnp.mean(grad, -1, keepdims=True)
+    second = jnp.mean(grad * normed, -1, keepdims=True)
+    return inverse * (grad - first - normed * second)
+
+
+def near_keys(rows, t):
+    return max(0, min(rows, REACH) - TILE * t)
+
+
+def by_row_tiles(rows, body):
+    def tile(i, _):
+        for part in range(0, TILE, 32):
+            body(pl.ds(aligned(i * TILE + part, 32), 32))
+        return 0
+
+    lax.fori_loop(0, rows // TILE, tile, 0)
+
+
+def border_rows(rows):
+    starts, found = {0}, {0}
+    while found:
+        found = {at + size for at in found for size in IMAGES if at + size < rows} - starts
+        starts |= found
+    reach = max(max(rows - at, at + size - rows) for at in starts for size in IMAGES if at < rows < at + size)
+    return min(rows, -(-reach // 16) * 16)
+
+
+def mark_segments(seg_ref, keys_ref, queries_ref, rows):
+    for at, size in chunks(rows, TILE):
+        column = jnp.broadcast_to(seg_ref[0:1, at : at + size].astype(F32), (TILE, size)).T
+        same = column == lax.broadcasted_iota(jnp.int32, (size, TILE), 1).astype(F32)
+        keys_ref[at : at + size, :] = jnp.where(same, 1.0, 0.0).astype(BF16)
+        queries_ref[at : at + size, :] = jnp.where(same, 0.0, NEG).astype(BF16)
+
+
+def both_rows(block):
+    return jnp.concatenate([block, block], 0)
+
+
+def with_marks(slab, marks):
+    return jnp.concatenate([slab, marks], 1)
+
+
+def shared_steps(sizes, most):
+    groups = []
+    for t, size in sorted(enumerate(sizes), key=lambda item: -item[1]):
+        if not size:
+            continue
+        for group in groups:
+            if sum(sizes[other] for other in group) + size <= most:
+                group.append(t)
+                break
+        else:
+            groups.append([t])
+    return groups
+
+
+def row_of(gain_ref):
+    return jnp.concatenate([gain_ref[i : i + 1, :] for i in range(gain_ref.shape[0])], 1)
+
+
+def norm_rows(x_ref, gain_ref, out_ref, rows, row_from=0):
+    def tile(i, _):
+        for part in range(0, 64, 32):
+            at = pl.ds(aligned(row_from + i * 64 + part, 32), 32)
+            normed, _ = standardize(x_ref[at, :].astype(F32))
+            out_ref[at, :] = (normed * row_of(gain_ref)).astype(BF16)
+        return 0
+
+    lax.fori_loop(0, rows // 64, tile, 0)
+
+
+def transpose_steps(src, base, into, row_from, count, width):
+    def one(c, at, part):
+        def step():
+            rows_here = pl.ds(row_from + at if isinstance(row_from, int) else aligned(row_from + at, 64), part)
+            into[c : c + TILE, at : at + part] = src[rows_here, base + c : base + c + TILE].T
+
+        return step
+
+    return [one(c, at, part) for c in range(0, width, TILE) for at, part in chunks(count, TILE)]
+
+
+def project(a_ref, w_ref, out_ref, width, at, after_values):
+    def one(c):
+        def step():
+            scale = 0.125 * LOG2E if c < width else 1.0
+            out_ref[at, c : c + 256] = (dot(a_ref[at, :], w_ref[:, c : c + 256]) * scale).astype(BF16)
+
+        return step
+
+    for c in range(2 * width, 3 * width, 256):
+        one(c)()
+    interleave([one(c) for c in range(0, 2 * width, 256)], after_values)
+
+
+def own_tile(t, tiles, me):
+    return (tiles - 1 - t) * (1 - me) + t * me
+
+
+def softmax_steps(items, scores_ref, probs_ref):
+    count = len(items)
+
+    def here(n, block, at, size):
+        return slice(block["off"] + at, block["off"] + at + size), slice((n % 2) * 256, (n % 2) * 256 + 256)
+
+    def scores(n):
+        def one(block):
+            def step():
+                scores_ref[block["lane"]][here(n, block, 0, block["size"])] = dot(block["k"](), block["q2"](), NT)
+
+            return step
+
+        return [one(block) for block in items[n]]
+
+    def largest(n):
+        steps = []
+        for block in items[n]:
+
+            def part(at, block=block):
+                def step():
+                    new = scores_ref[block["lane"]][here(n, block, at, 32)]
+                    block["max"] = jnp.maximum(block["max"], new) if at else new
+
+                return step
+
+            def last(block=block):
+                top = jnp.max(block["max"], 0, keepdims=True)
+                was = block["top"]()
+                block["max"] = top if was is None else jnp.maximum(top, was)
+
+            steps += [part(at) for at in range(0, block["size"], 32)] + [last]
+        return steps
+
+    def exponentials(n):
+        def part(block, at, size):
+            def step():
+                s = scores_ref[block["lane"]][here(n, block, at, size)]
+                probs_ref[block["lane"]][here(n, block, at, size)] = jnp.exp2(s - block["max"]).astype(BF16)
+
+            return step
+
+        return [part(block, at, size) for block in items[n] for at, size in chunks(block["size"], 64)]
+
+    def values(n):
+        def one(block):
+            def step():
+                vt = jnp.concatenate([block["vt"](), jnp.ones((16, block["size"]), BF16)], 0)
+                mix = dot(vt, probs_ref[block["lane"]][here(n, block, 0, block["size"])])
+                block["end"](block["max"], mix[TILE : TILE + 1, :], own_halves(mix))
+
+            return step
+
+        return [one(block) for block in items[n]]
+
+    for step in scores(0) + largest(0):
+        step()
+    for n in range(count):
+        interleave(scores(n + 1) if n + 1 < count else [], exponentials(n))
+        interleave(values(n), largest(n + 1) if n + 1 < count else [])
+
+
+def attend_local(r, rows, width):
+    tiles, half_pairs = rows // TILE, width // TILE // 2
+
+    def two_pairs(first, _):
+        def one(k, u):
+            hp = first + k * half_pairs
+            lane = lambda base: pl.ds(aligned(base + hp * TILE, TILE), TILE)
+            row_u = slice(u * TILE, u * TILE + TILE)
+
+            def end(top, total, mix):
+                r.top[pl.ds(hp * tiles + u, 1), :] = top
+                r.total[pl.ds(hp * tiles + u, 1), :] = total
+                r.gf[row_u, lane(0)] = mix
+
+            return dict(
+                size=rows, off=0, lane=k, top=lambda: None, end=end,
+                q2=lambda: with_marks(pair_rows(r.pv[row_u, lane(0)]), both_rows(r.seg_q[row_u, :])),
+                k=lambda: with_marks(r.pv[:, lane(width)], r.seg_k[...]),
+                vt=lambda: r.act_t[lane(0), :rows],
+            )
+
+        softmax_steps([[one(k, u) for k in range(2)] for u in range(tiles)], (r.h, r.ga), (r.act, r.gh))
+        return 0
+
+    lax.fori_loop(0, half_pairs, two_pairs, 0)
+
+
+def attend_cross(r, me, rows, width):
+    tiles, half_pairs = rows // TILE, width // TILE // 2
+    sizes = [near_keys(rows, t) for t in range(tiles)]
+
+    def two_pairs(first, _):
+        def one(k, t, off):
+            hp = first + k * half_pairs
+            lane = lambda base: pl.ds(aligned(base + hp * TILE, TILE), TILE)
+            size = sizes[t]
+            u = own_tile(t, tiles, me)
+            i = hp * tiles + u
+            keys = pl.ds(aligned((rows - size) * me, 64), size)
+            lanes = pl.ds(aligned(TILE * t * me, TILE), size)
+
+            def end(top, total, mix):
+                top_was, total_was = r.top[pl.ds(i, 1), :], r.total[pl.ds(i, 1), :]
+                fade = jnp.exp2(top_was - top)
+                total = total_was * fade + total
+                over = 1.0 / total
+                half = TILE // 2
+                by_head = lambda row: jnp.concatenate(
+                    [jnp.broadcast_to(row[:, :TILE], (half, TILE)), jnp.broadcast_to(row[:, TILE:], (half, TILE))], 0
+                )
+                done = (r.gf[tile_at(u), lane(0)] * by_head(fade) + mix) * by_head(over)
+                r.mixedv[tile_at(u), lane(0)] = done.T.astype(BF16)
+                r.stats[0, pl.ds(hp * tiles + t, 1), :] = top + jnp.log2(total)
+
+            return dict(
+                size=size, off=off, lane=k, top=lambda: r.top[pl.ds(i, 1), :], end=end,
+                q2=lambda: with_marks(pair_rows(r.pv[tile_at(u), lane(0)]), both_rows(r.seg_q[tile_at(u), :])),
+                k=lambda: with_marks(r.prv[keys, lane(width)], r.seg_kr[keys, :]),
+                vt=lambda: r.act_t[pl.ds(aligned(width + hp * TILE, TILE), TILE), lanes],
+            )
+
+        items = []
+        for group in shared_steps(sizes, rows):
+            offs = [sum(sizes[other] for other in group[:n]) for n in range(len(group))]
+            items.append([one(k, t, off) for t, off in zip(group, offs) for k in range(2)])
+        softmax_steps(items, (r.h, r.ga), (r.act, r.gh))
+
+        for t in range(tiles):
+            if not sizes[t]:
+                for k in range(2):
+                    no_neighbour(first + k * half_pairs, t)
+        return 0
+
+    def no_neighbour(hp, t):
+        lane = pl.ds(aligned(hp * TILE, TILE), TILE)
+        u = own_tile(t, tiles, me)
+        i = hp * tiles + u
+        total = r.total[pl.ds(i, 1), :]
+        over = 1.0 / total
+        half = TILE // 2
+        scale = jnp.concatenate(
+            [jnp.broadcast_to(over[:, :TILE], (half, TILE)), jnp.broadcast_to(over[:, TILE:], (half, TILE))], 0
+        )
+        r.mixedv[tile_at(u), lane] = (r.gf[tile_at(u), lane] * scale).T.astype(BF16)
+        r.stats[0, pl.ds(hp * tiles + t, 1), :] = r.top[pl.ds(i, 1), :] + jnp.log2(total)
+
+    lax.fori_loop(0, half_pairs, two_pairs, 0)
+
+
+INV_SQRT2PI = 1.0 / math.sqrt(2.0 * math.pi)
+TAIL_SLOPE = 0.3275911 * math.sqrt(0.5)
+TAIL = tuple(0.5 * c for c in (0.254829592, -0.284496736, 1.421413741, -1.453152027, 1.061405429))
+
+
+def gelu_parts(h):
+    below_one = 1.0 + TAIL_SLOPE * jnp.abs(h)
+    t = pl.reciprocal(below_one, approx=True)
+    t = t * (2.0 - below_one * t)
+    bell = jnp.exp2(h * h * (-0.5 * LOG2E))
+    poly = TAIL[4]
+    for c in TAIL[3::-1]:
+        poly = poly * t + c
+    tail = poly * t * bell
+    below = jnp.where(h < 0.0, tail, 1.0 - tail)
+    return below, below + h * bell * INV_SQRT2PI
+
+
+def where_am_i():
+    dp, blk = lax.axis_index("dp"), lax.axis_index("blk")
+    bits = {name: lax.rem(lax.div(dp, 2**k), 2) for k, name in enumerate(BITS[:-1])}
+    bits["y"] = blk
+    return dp, blk, bits
+
+
+def partner_of(name, dp, blk, bits):
+    if name == "y":
+        return {"blk": 1 - blk}
+    return {"dp": dp + 2 ** BITS.index(name) * (1 - 2 * bits[name])}
+
+
+def block_index(order, d, y):
+    bits = {name: (d >> k) & 1 for k, name in enumerate(BITS[:-1])}
+    bits["y"] = y
+    index = 0
+    for name in order:
+        index = 2 * index + bits[name]
+    return index
+
+
+class Reducer:
+    def __init__(self, r):
+        self.r = r
+        self.dp, self.blk, self.bits = where_am_i()
+
+    def keep(self, order, stage):
+        base = 0
+        for k in range(stage + 1):
+            base = base + self.bits[order[k]] * (16 >> k)
+        return base
+
+    def copy(self, chunk, stage):
+        number, unit, units, order, _ = chunk
+        half = 16 >> stage
+        base = self.keep(order, stage - 1) if stage else 0
+        away = base + (1 - self.bits[order[stage]]) * half
+        slot = 32 - 2 * half
+        return pltpu.make_async_remote_copy(
+            src_ref=self.r.g.at[pl.ds(unit, units), pl.ds(away, half)],
+            dst_ref=self.r.recv.at[pl.ds(unit, units), pl.ds(slot, half)],
+            send_sem=self.r.rs_sent.at[number, stage],
+            recv_sem=self.r.rs_got.at[number, stage],
+            device_id=partner_of(order[stage], self.dp, self.blk, self.bits),
+            device_id_type=MESH,
+        )
+
+    def start(self, chunk, stage=0):
+        self.copy(chunk, stage).start()
+
+    def finish(self, chunk, stage):
+        number, unit, units, order, write = chunk
+        half = 16 >> stage
+        self.copy(chunk, stage).wait()
+        keep = self.keep(order, stage)
+        slot = 32 - 2 * half
+        if stage == 4:
+            for k in range(units):
+                write(k, self.r.g[unit + k, keep].astype(F32) + self.r.recv[unit + k, slot].astype(F32))
+            return
+        step = min(half, 4)
+
+        def add(j, _):
+            for k in range(units):
+                mine = pl.ds(keep + j * step, step)
+                self.r.g[unit + k, mine] += self.r.recv[unit + k, pl.ds(slot + j * step, step)]
+            return 0
+
+        if half == step:
+            add(0, 0)
+        else:
+            lax.fori_loop(0, half // step, add, 0)
+        self.start(chunk, stage + 1)
+
+
+def kernel_layer(names, *refs):
+    r = SimpleNamespace(**dict(zip(names, refs)))
+    rows, width = r.xv.shape
+    ff = r.wb.shape[0]
+    me = lax.axis_index("blk")
+    reach, tiles, pairs = min(rows, REACH), rows // TILE, width // TILE
+    red = Reducer(r)
+    dp, blk, bits = red.dp, red.blk, red.bits
+
+    barrier = pltpu.get_barrier_semaphore()
+    for name in BITS:
+        pl.semaphore_signal(
+            barrier, inc=1, device_id=partner_of(name, dp, blk, bits), device_id_type=MESH
+        )
+    loads = {}
+    for k, (src, into) in enumerate(
+        [("x", r.xv), ("w_qkv", r.wa.at[:, : 3 * width]), ("w_out", r.wo), ("cot", r.cotv), ("w_down", r.wb)]
+    ):
+        loads[src] = pltpu.make_async_copy(getattr(r, src), into, r.loads.at[k])
+        loads[src].start()
+    loads["w_up"] = pltpu.make_async_copy(r.w_up, r.wa, r.loads.at[5])
+    load_w_qkv = pltpu.make_async_copy(r.w_qkv, r.wa.at[:, : 3 * width], r.loads.at[6])
+    near, span = rows // 2, border_rows(rows)
+    far = pl.ds(aligned(span * (1 - me), 16), rows - span)
+    give = pl.ds(aligned((rows - span) * (1 - me), 16), span)
+    give_near = pl.ds(aligned((rows - near) * (1 - me), 16), near)
+    give_far = pl.ds(aligned((rows - span) * (1 - me) + near * me, 16), span - near)
+    to_y = dict(device_id={"blk": 1 - me}, device_id_type=MESH)
+    if span < rows:
+        r.xr[far, :] = jnp.zeros((rows - span, width), BF16)
+        r.gmr[far, :] = jnp.zeros((rows - span, width), BF16)
+    loads["x"].wait()
+    pl.semaphore_wait(barrier, len(BITS))
+
+    def to_neighbour(k, src, dst):
+        copy = pltpu.make_async_remote_copy(
+            src_ref=src, dst_ref=dst, send_sem=r.sent.at[k], recv_sem=r.got.at[k], **to_y
+        )
+        copy.start()
+        return copy
+
+    send_near = to_neighbour(0, r.xv.at[give_near], r.xr.at[give_near])
+    send_seg = to_neighbour(1, r.seg, r.segr)
+    send_far = to_neighbour(4, r.xv.at[give_far], r.xr.at[give_far])
+    norm_rows(r.xv, r.gain_attn, r.ffn_in, rows)
+    mark_segments(r.seg, r.seg_k, r.seg_q, rows)
+    loads["w_qkv"].wait()
+    project(r.ffn_in, r.wa, r.pv, width, slice(None), transpose_steps(r.pv, 2 * width, r.act_t, 0, rows, width))
+    attend_local(r, rows, width)
+
+    send_seg.wait()
+    mark_segments(r.segr, r.seg_kr, r.seg_qr, rows)
+
+    def neighbour_half(n, _):
+        pl.when(n == 0)(send_near.wait)
+        pl.when(n == 1)(send_far.wait)
+        row_from = near * (me * (1 - n) + (1 - me) * n)
+        norm_rows(r.xr, r.gain_attn, r.ffn_in, near, row_from)
+        project(r.ffn_in, r.wa, r.prv, width, pl.ds(aligned(row_from, 64), near), [])
+        return 0
+
+    lax.fori_loop(0, 2, neighbour_half, 0)
+    loads["w_up"].start()
+    for step in transpose_steps(r.prv, 2 * width, r.act_t.at[width : 2 * width, :], (rows - reach) * me, reach, width):
+        step()
+    attend_cross(r, me, rows, width)
+
+    block_rows = width // 16
+
+    def put(unit, order, d, y, row, block):
+        r.g[unit, block_index(order, d, y), row : row + block.shape[0], :] = block
+
+    def into(ref, base):
+        def write(k, block):
+            ref[:, tile_at(base + k)] = block
+
+        return write
+
+
+    def up_unit(i, k):
+        return lax.div(i, 2) * 4 + 2 * k + lax.rem(i, 2) if not isinstance(i, int) else i // 2 * 4 + 2 * k + i % 2
+
+    def chunk_up(c, k):
+        def write(m, block):
+            r.o_up[:, tile_at(4 * c + 2 * m + k)] = block
+
+        return (2 * c + k, 4 * c + 2 * k, 2, ORDERS[k], write)
+
+    def chunk_down(j):
+        def write(k, block):
+            r.o_down[k * block_rows : (k + 1) * block_rows, j * UNIT : (j + 1) * UNIT] = block
+
+        return (6 + j, 12 + 4 * j, 4, ORDERS[6 + j], write)
+
+    out_chunk = (9, 0, 3, ORDERS[9], into(r.o_out, 0))
+
+    middle_chunk = (10, 6, 3, ORDERS[10], into(r.o_qkv, 3))
+
+    def chunk_qkv(n, k):
+        j = n + 6 * k
+        return (11 + 2 * n + k, 3 + j, 1, ORDERS[11 + k], into(r.o_qkv, j))
+
+    table = [chunk_up(c, k) for c in range(3) for k in range(2)] + [chunk_down(j) for j in range(3)]
+    table += [out_chunk, middle_chunk] + [chunk_qkv(n, k) for n in range(3) for k in range(2)]
+
+    def ends(name, step):
+        for chunk, stage in ENDS.get((name, step), ()):
+            red.finish(table[chunk], stage)
+
+    def ends_in_loop(name, index, steps):
+        for step in steps:
+            if (name, step) in ENDS:
+                pl.when(index == step)(lambda step=step: ends(name, step))
+
+    loads["w_out"].wait()
+    for c, part in chunks(width, 256):
+        r.mid[:, c : c + part] = r.xv[:, c : c + part].astype(F32) + dot(r.mixedv[...], r.wo[:, c : c + part])
+
+    def norm_two(at):
+        normed, _ = standardize(r.mid[at, :])
+        r.ffn_in[at, :] = (normed * row_of(r.gain_ffn)).astype(BF16)
+        r.lo[at, :] = r.mid[at, :]
+        r.gf[at, :] = jnp.zeros_like(r.gf[at, :])
+
+    norm_two_steps = [lambda at=at: norm_two(slice(at, at + 32)) for at in range(0, rows, 32)]
+    norm_two_steps += transpose_steps(r.ffn_in, 0, r.ffn_t, 0, rows, width)
+    for src in ("w_up", "cot", "w_down"):
+        loads[src].wait()
+
+    def column(n, i):
+        return pl.ds(aligned((n % 2) * (ff // 2) + i * 256, 256), 256)
+
+    def side(n):
+        return slice((n % 2) * 256, (n % 2) * 256 + 256)
+
+    def ff_before(n, i):
+        def up():
+            r.h[:, side(n)] = dot(r.ffn_in[...], r.wa[:, column(n, i)])
+
+        def down():
+            r.ga[:, side(n)] = dot(r.cotv[...], r.wb[column(n, i), :], NT)
+
+        return [up, down]
+
+    def ff_during(n):
+        def part(row):
+            def step():
+                tile = slice(row, row + 32)
+                h = r.h[tile, side(n)]
+                below, slope = gelu_parts(h)
+                r.act[tile, side(n)] = (h * below).astype(BF16)
+                r.gh[tile, side(n)] = (slope * r.ga[tile, side(n)]).astype(BF16)
+
+            return step
+
+        return [part(row) for row in range(0, rows, 32)]
+
+    def ff_after(n, i):
+        def out(c):
+            def step():
+                r.lo[:, c : c + 256] += dot(r.act[:, side(n)], r.wb[column(n, i), c : c + 256])
+
+            return step
+
+        def back(c):
+            def step():
+                r.gf[:, c : c + 256] += dot(r.gh[:, side(n)], r.wa[c : c + 256, column(n, i)], NT)
+
+            return step
+
+        def weights():
+            grad = dot(r.ffn_t[...], r.gh[:, side(n)]).astype(BF16)
+            for d in range(16):
+                for k in range(2):
+                    put(up_unit(i, k), ORDERS[k], d, n % 2, 0,
+                        grad[d * block_rows : (d + 1) * block_rows, k * UNIT : (k + 1) * UNIT])
+
+        def turn():
+            base = (n % 2) * (ff // 2) + i * 256
+            for c in range(0, 256, TILE):
+                for row in range(0, rows, TILE):
+                    r.act_t[pl.ds(aligned(base + c, TILE), TILE), row : row + TILE] = r.act[
+                        row : row + TILE, (n % 2) * 256 + c : (n % 2) * 256 + c + TILE].T
+
+        return [weights] + [step(c) for step in (out, back) for c in range(0, width, 256)] + [turn]
+
+    last = ff // 512 - 1
+    interleave([ff_before(0, 0)[1], ff_before(1, 0)[1]], norm_two_steps)
+    ff_before(0, 0)[0]()
+    interleave(ff_before(1, 0)[:1], ff_during(0))
+
+    def ff_two(i, _):
+        interleave(ff_after(0, i) + ff_before(0, i + 1), ff_during(1))
+        interleave(ff_after(1, i) + ff_before(1, i + 1), ff_during(0))
+
+        @pl.when(lax.rem(i, 2) == 1)
+        def _():
+            for k in range(2):
+                red.start(chunk_up(lax.div(i, 2), k))
+
+        ends_in_loop("ff", i, range(last))
+        return 0
+
+    lax.fori_loop(0, last, ff_two, 0)
+    interleave(ff_after(0, last), ff_during(1))
+    for step in ff_after(1, last):
+        step()
+    for k in range(2):
+        red.start(chunk_up(last // 2, k))
+    ends("ff", last)
+    load_w_qkv.start()
+    out_lo = pltpu.make_async_copy(r.lo, r.layer_out, r.loads.at[7])
+    out_lo.start()
+
+    def grad_down(j):
+        order = ORDERS[6 + j]
+
+        def part(c):
+            def step():
+                both = jnp.concatenate(
+                    [r.cotv[:, half * (width // 2) + j * UNIT : half * (width // 2) + (j + 1) * UNIT]
+                     for half in range(2)], 1)
+                grad = dot(r.act_t[c : c + width, :], both).astype(BF16)
+                for part in range(4):
+                    for k in range(4):
+                        for half in range(2):
+                            at = part * 4 * block_rows + k * block_rows
+                            put(12 + 4 * j + k, order, 4 * (c // width) + part, half, 0,
+                                grad[at : at + block_rows, half * UNIT : (half + 1) * UNIT])
+
+            return step
+
+        return [part(c) for c in range(0, ff, width)]
+
+    r.gains[...] = jnp.zeros_like(r.gains)
+
+    def norm_two_back(at):
+        def step():
+            normed, inverse = standardize(r.mid[at, :])
+            grad = r.gf[at, :]
+            r.gains[0:8, :] += fold_sum(grad * normed)
+            grad = r.cotv[at, :].astype(F32) + norm_backward(
+                grad * row_of(r.gain_ffn), normed, inverse
+            )
+            r.gf[at, :] = grad
+            r.ffn_in[at, :] = grad.astype(BF16)
+
+        return step
+
+    def norm_one_again(at):
+        def step():
+            normed, _ = standardize(r.xv[at, :].astype(F32))
+            r.xr[at, :] = (normed * row_of(r.gain_attn)).astype(BF16)
+
+        return step
+
+    row_tiles = [slice(at, at + 32) for at in range(0, rows, 32)]
+    beside = [
+        [norm_two_back(at) for at in row_tiles],
+        [norm_one_again(at) for at in row_tiles] + transpose_steps(r.mixedv, 0, r.ffn_t, 0, rows, width),
+        transpose_steps(r.xr, 0, r.n1_t, 0, rows, width) + transpose_steps(r.pv, width, r.kt, 0, rows, width)
+        + transpose_steps(r.prv, width, r.ktr, (rows - reach) * me, reach, width),
+    ]
+    for j in range(3):
+        for n, step in enumerate(grad_down(j)):
+            share = beside[j][n * len(beside[j]) // 4 : (n + 1) * len(beside[j]) // 4]
+            pl.when(me >= 0)(lambda step=step, share=share: interleave([step], share))
+        red.start(chunk_down(j))
+        ends("dn", j)
+
+    for c, part in chunks(width, 256):
+        r.gm[:, c : c + part] = dot(r.ffn_in[...], r.wo[c : c + part, :], NT).astype(BF16)
+    send_gm = to_neighbour(2, r.gm.at[give], r.gmr.at[give])
+    ends("gm", 0)
+
+    def delta_rows(hp, _):
+        lane = tile_at(hp)
+        half = TILE // 2
+        for t in range(tiles):
+            at = tile_at(own_tile(t, tiles, me))
+            both = (r.gm[at, lane].astype(F32) * r.mixedv[at, lane].astype(F32)).T
+            first = jnp.sum(both[:half, :], 0, keepdims=True)
+            second = jnp.sum(both[half:, :], 0, keepdims=True)
+            r.stats[1, pl.ds(hp * tiles + t, 1), :] = jnp.concatenate([first, second], 1)
+        return 0
+
+    lax.fori_loop(0, pairs, delta_rows, 0)
+    send_stats = to_neighbour(3, r.stats, r.statsr)
+    ends("de", 0)
+
+    out_lo.wait()
+
+    def grad_steps(items):
+        def here(n, block, at, size):
+            return slice(block["off"] + at, block["off"] + at + size), side(n)
+
+        def before(n):
+            def scores(block):
+                def step():
+                    r.h[here(n, block, 0, block["size"])] = dot(block["k"](), block["q2"](), NT)
+
+                return step
+
+            def probs(block):
+                def step():
+                    r.ga[here(n, block, 0, block["size"])] = dot(block["v"](), block["do2"](), NT)
+
+                return step
+
+            return [step(block) for block in items[n] for step in (scores, probs)]
+
+        def during(n):
+            def part(block, at, size):
+                def step():
+                    rows_here = here(n, block, at, size)
+                    p = jnp.exp2(r.h[rows_here] - block["lse"]())
+                    r.act[rows_here] = p.astype(BF16)
+                    r.gh[rows_here] = (p * (r.ga[rows_here] - block["delta"]())).astype(BF16)
+
+                return step
+
+            return [part(block, at, size) for block in items[n] for at, size in chunks(block["size"], 64)]
+
+        def after(n):
+            steps = []
+            for block in items[n]:
+                rows_here = here(n, block, 0, block["size"])
+                steps += block["after"](lambda at=rows_here: r.act[at], lambda at=rows_here: r.gh[at])
+            return steps
+
+        count = range(len(items))
+        pipeline([before(n) for n in count], [during(n) for n in count], [after(n) for n in count])
+
+    sizes = [near_keys(rows, t) for t in range(tiles)]
+    groups = shared_steps(sizes, rows)
+
+    def offsets(group):
+        return [(t, sum(sizes[other] for other in group[:n])) for n, t in enumerate(group)]
+
+    def own_queries(hp):
+        lane = lambda base: pl.ds(aligned(base + hp * TILE, TILE), TILE)
+        parts = [[] for _ in range(tiles)]
+
+        def base(t):
+            at_u = tile_at(own_tile(t, tiles, me))
+            return dict(
+                q2=lambda: with_marks(pair_rows(r.pv[at_u, lane(0)]), both_rows(r.seg_q[at_u, :])),
+                do2=lambda: pair_rows(r.gm[at_u, lane(0)]),
+                lse=lambda: r.stats[0, pl.ds(hp * tiles + t, 1), :],
+                delta=lambda: r.stats[1, pl.ds(hp * tiles + t, 1), :],
+            )
+
+        def add_queries(t, new):
+            parts[t].append(new)
+            if len(parts[t]) == (2 if sizes[t] else 1):
+                dq = own_halves(sum(parts[t][1:], parts[t][0])) * 0.125
+                r.mixedv[tile_at(own_tile(t, tiles, me)), lane(0)] = dq.T.astype(BF16)
+
+        def local(t):
+            mine = base(t)
+
+            def after(p, ds):
+                def queries():
+                    add_queries(t, dot(r.kt[lane(0), :], ds()))
+
+                def values():
+                    new = dot(p(), mine["do2"]())
+                    r.mid[:, lane(0)] = new if t == 0 else r.mid[:, lane(0)] + new
+
+                def keys():
+                    new = dot(ds(), pair_rows(r.pv[tile_at(own_tile(t, tiles, me)), lane(0)]))
+                    r.lo[:, lane(0)] = new if t == 0 else r.lo[:, lane(0)] + new
+
+                return [queries, values, keys]
+
+            return dict(mine, size=rows, off=0, after=after, v=lambda: r.pv[:, lane(2 * width)],
+                        k=lambda: with_marks(r.pv[:, lane(width)], r.seg_k[...]))
+
+        def cross(t, off):
+            keys = pl.ds(aligned((rows - sizes[t]) * me, 64), sizes[t])
+            lanes = pl.ds(aligned(TILE * t * me, TILE), sizes[t])
+
+            def after(p, ds):
+                def queries():
+                    add_queries(t, dot(r.ktr[lane(0), lanes], ds()))
+
+                return [queries]
+
+            return dict(base(t), size=sizes[t], off=off, after=after, v=lambda: r.prv[keys, lane(2 * width)],
+                        k=lambda: with_marks(r.prv[keys, lane(width)], r.seg_kr[keys, :]))
+
+        items = []
+        for t in range(tiles):
+            items.append([local(t)])
+            if t < len(groups):
+                items.append([cross(other, off) for other, off in offsets(groups[t])])
+        grad_steps(items)
+
+    def other_queries(hp):
+        lane = lambda base: pl.ds(aligned(base + hp * TILE, TILE), TILE)
+
+        def block(t, off):
+            at_u = tile_at(t * (1 - me) + (tiles - 1 - t) * me)
+            keys = pl.ds(aligned((rows - sizes[t]) * (1 - me), 64), sizes[t])
+
+            def after(p, ds):
+                def values():
+                    r.mid[keys, lane(0)] += dot(p(), pair_rows(r.gmr[at_u, lane(0)]))
+
+                def scores():
+                    r.lo[keys, lane(0)] += dot(ds(), pair_rows(r.prv[at_u, lane(0)]))
+
+                return [values, scores]
+
+            return dict(
+                size=sizes[t], off=off, after=after,
+                q2=lambda: with_marks(pair_rows(r.prv[at_u, lane(0)]), both_rows(r.seg_qr[at_u, :])),
+                do2=lambda: pair_rows(r.gmr[at_u, lane(0)]),
+                lse=lambda: r.statsr[0, pl.ds(hp * tiles + t, 1), :],
+                delta=lambda: r.statsr[1, pl.ds(hp * tiles + t, 1), :],
+                k=lambda: with_marks(r.pv[keys, lane(width)], r.seg_k[keys, :]),
+                v=lambda: r.pv[keys, lane(2 * width)],
+            )
+
+        grad_steps([[block(t, off) for t, off in offsets(group)] for group in groups])
+        r.pv[:, lane(width)] = (r.lo[:, lane(0)] * (1.0 / LOG2E)).astype(BF16)
+        r.pv[:, lane(2 * width)] = r.mid[:, lane(0)].astype(BF16)
+
+    def own_pass(hp, _):
+        own_queries(hp)
+        ends_in_loop("own", hp, range(pairs))
+        return 0
+
+    lax.fori_loop(0, OUT_AFTER, own_pass, 0)
+    for n, name in enumerate(BITS):
+        pl.semaphore_signal(
+            r.again.at[n], inc=1, device_id=partner_of(name, dp, blk, bits), device_id_type=MESH
+        )
+
+    for c, part in chunks(width, 256):
+        grad = dot(r.ffn_t[...], r.ffn_in[:, c : c + part]).astype(BF16)
+        for k in range(2):
+            column_at = c + k * UNIT
+            y, unit = column_at // (width // 2), column_at % (width // 2) // UNIT
+            for d in range(16):
+                put(unit, ORDERS[9], d, y, 0,
+                    grad[d * block_rows : (d + 1) * block_rows, k * UNIT : (k + 1) * UNIT])
+    for k in range(len(BITS)):
+        pl.semaphore_wait(r.again.at[k], 1)
+    red.start(out_chunk)
+    ends("out", 0)
+    lax.fori_loop(OUT_AFTER, pairs, own_pass, 0)
+
+    send_gm.wait()
+    send_stats.wait()
+    r.pv[:, :width] = r.mixedv[...]
+
+    def grad_qkv(j, order):
+        columns = [pl.ds(aligned(y * (3 * width // 2) + j * UNIT, UNIT), UNIT) for y in range(2)]
+        grad = dot(r.n1_t[...], jnp.concatenate([r.pv[:, at] for at in columns], 1)).astype(BF16)
+        for y in range(2):
+            for d in range(16):
+                put(3 + j, order, d, y, 0,
+                    grad[d * block_rows : (d + 1) * block_rows, y * UNIT : (y + 1) * UNIT])
+
+    half_pairs = pairs // 2
+
+    def first_pass(hp, _):
+        other_queries(hp)
+        grad_qkv(half_pairs + hp, ORDERS[10])
+
+        @pl.when(hp == half_pairs - 1)
+        def _():
+            red.start(middle_chunk)
+
+        ends_in_loop("oth", hp, range(half_pairs))
+        return 0
+
+    lax.fori_loop(0, half_pairs, first_pass, 0)
+
+    def second_pass(hp, _):
+        other_queries(hp)
+        for k in range(2):
+            grad_qkv(hp - half_pairs + 6 * k, ORDERS[11 + k])
+            red.start(chunk_qkv(hp - half_pairs, k))
+        ends_in_loop("oth", hp, range(half_pairs, pairs))
+        return 0
+
+    lax.fori_loop(half_pairs, pairs, second_pass, 0)
+
+    load_w_qkv.wait()
+    for c, part in chunks(width, 256):
+        r.lo[:, c : c + part] = dot(r.pv[...], r.wa[c : c + part, : 3 * width], NT)
+    ends("tail", 0)
+
+    def norm_one_back(at):
+        normed, inverse = standardize(r.xv[at, :].astype(F32))
+        grad = r.lo[at, :]
+        r.gains[8:16, :] += fold_sum(grad * normed)
+        r.mid[at, :] = r.gf[at, :] + norm_backward(
+            grad * row_of(r.gain_attn), normed, inverse
+        )
+
+    by_row_tiles(rows, norm_one_back)
+    ends("tail", 1)
+    out_gin = pltpu.make_async_copy(r.mid, r.input_grad, r.loads.at[8])
+    out_gin.start()
+    r.o_gains[0] = jnp.concatenate(
+        [jnp.sum(r.gains[0:8, :], 0, keepdims=True), jnp.sum(r.gains[8:16, :], 0, keepdims=True),
+         jnp.zeros((6, width), F32)], 0)
+
+    def gain_copy(k):
+        return pltpu.make_async_remote_copy(
+            src_ref=r.o_gains.at[k], dst_ref=r.gains_in.at[k], send_sem=r.gain_sent.at[k], recv_sem=r.gain_got.at[k],
+            device_id=partner_of(ORDER_A[k], dp, blk, bits), device_id_type=MESH)
+
+    gain_copy(0).start()
+    for k in range(5):
+        ends("tail", 2 + k)
+        gain_copy(k).wait()
+        r.o_gains[k + 1] = r.o_gains[k] + r.gains_in[k]
+        if k + 1 < 5:
+            gain_copy(k + 1).start()
+    ends("tail", 7)
+    out_gin.wait()
+
+
+def call_layer(x, seg, gain_attn, gain_ffn, w_qkv, w_out, w_up, w_down, cot):
+    rows, width = x.shape
+    ff = w_down.shape[0]
+    tiles, pairs, block = rows // TILE, width // TILE, width // 16
+    stat = (-(-pairs * tiles // 8) * 8, 2 * TILE)
+    vmem = pl.BlockSpec(memory_space=pltpu.VMEM)
+    anywhere = pl.BlockSpec(memory_space=pl.ANY)
+    ins = dict(x=anywhere, seg=vmem, gain_attn=vmem, gain_ffn=vmem, w_qkv=anywhere, w_out=anywhere,
+               w_up=anywhere, w_down=anywhere, cot=anywhere)
+    outs = dict(
+        layer_out=((rows, width), F32, anywhere), input_grad=((rows, width), F32, anywhere),
+        o_gains=((6, 8, width), F32, vmem), o_qkv=((block, 3 * width // 2), F32, vmem),
+        o_out=((block, width // 2), F32, vmem), o_up=((block, ff // 2), F32, vmem),
+        o_down=((ff // 16, width // 2), F32, vmem),
+    )
+    big = ((rows, width), BF16)
+    wide = ((rows, width), F32)
+    scratch = dict(
+        xv=big, xr=big, mixedv=big, cotv=big, pv=((rows, 3 * width), BF16), prv=((rows, 3 * width), BF16),
+        wo=((width, width), BF16), wa=((width, ff), BF16), wb=((ff, width), BF16),
+        mid=wide, lo=wide, gf=wide, ffn_in=big, ffn_t=((width, rows), BF16), act_t=((ff, rows), BF16),
+        h=((rows, 512), F32), ga=((rows, 512), F32), act=((rows, 512), BF16), gh=((rows, 512), BF16),
+        gmr=big, stats=((2,) + stat, F32), statsr=((2,) + stat, F32), top=(stat, F32), total=(stat, F32),
+        segr=((1, rows), jnp.int32), seg_k=((rows, TILE), BF16), seg_q=((rows, TILE), BF16),
+        seg_kr=((rows, TILE), BF16), seg_qr=((rows, TILE), BF16),
+        gains=((16, width), F32), gains_in=((5, 8, width), F32),
+        g=((24, 32, block, UNIT), BF16), recv=((24, 31, block, UNIT), BF16),
+    )
+    sems = dict(loads=(9,), sent=(5,), got=(5,), rs_sent=(17, 5), rs_got=(17, 5), gain_sent=(5,), gain_got=(5,))
+    names = list(ins) + list(outs) + list(scratch) + list(sems) + ["again"]
+
+    def body(*refs):
+        r = dict(zip(names, refs))
+        wb = r["wb"]
+        extra = dict(
+            kt=wb.at[0:width, 0:rows], ktr=wb.at[width : 2 * width, 0:rows],
+            n1_t=wb.at[2 * width : 3 * width, 0:rows], gm=wb.at[3 * width : 3 * width + rows, :],
+        )
+        kernel_layer(list(r) + list(extra), *r.values(), *extra.values())
+
+    return pl.pallas_call(
+        body,
+        out_shape=[jax.ShapeDtypeStruct(v[0], v[1]) for v in outs.values()],
+        in_specs=list(ins.values()),
+        out_specs=[v[2] for v in outs.values()],
+        scratch_shapes=[pltpu.VMEM(*v) for v in scratch.values()]
+        + [pltpu.SemaphoreType.DMA(n) for n in sems.values()]
+        + [pltpu.SemaphoreType.REGULAR((len(BITS),))],
+        compiler_params=pltpu.CompilerParams(
+            collective_id=0, has_side_effects=True, vmem_limit_bytes=60 * 2**20
+        ),
+        name="layer",
+    )(x, seg, gain_attn, gain_ffn, w_qkv, w_out, w_up, w_down, cot)
 
 
 def padded(block, sides, width):
@@ -248,30 +1286,71 @@
     )
 
 
+def copy_kernel(count, *refs):
+    source, target, held = refs[:count], refs[count : 2 * count], refs[2 * count : 3 * count]
+    sems = refs[3 * count]
+    pieces = []
+    for k in range(count):
+        rows = source[k].shape[0]
+        step = rows // 4 if rows % 64 == 0 else rows
+        pieces += [(k, pl.ds(at, step)) for at in range(0, rows, step)]
+    loads = [pltpu.make_async_copy(source[k].at[at], held[k].at[at], sems.at[0, n]) for n, (k, at) in enumerate(pieces)]
+    stores = [pltpu.make_async_copy(held[k].at[at], target[k].at[at], sems.at[1, n]) for n, (k, at) in enumerate(pieces)]
+    for copy in loads:
+        copy.start()
+    for load, store in zip(loads, stores):
+        load.wait()
+        store.start()
+    for copy in stores:
+        copy.wait()
+
+
+def copy_out(arrays):
+    anywhere = pl.BlockSpec(memory_space=pl.ANY)
+    return pl.pallas_call(
+        partial(copy_kernel, len(arrays)),
+        out_shape=[jax.ShapeDtypeStruct(a.shape, a.dtype) for a in arrays],
+        in_specs=[anywhere] * len(arrays),
+        out_specs=[anywhere] * len(arrays),
+        scratch_shapes=[pltpu.VMEM(a.shape, a.dtype) for a in arrays]
+        + [pltpu.SemaphoreType.DMA((2, 4 * len(arrays)))],
+        name="copy_out",
+    )(*arrays)
+
+
+def fast(tokens, segment_ids, gain_attn, w_qkv, w_out, gain_ffn, w_up, w_down, cotangent):
+    x, cot = tokens[0], cotangent[0]
+    rows, width = x.shape
+    layer_out, input_grad, gains, g_qkv, g_out, g_up, g_down = call_layer(
+        x, segment_ids, gain_attn.reshape(-1, TILE), gain_ffn.reshape(-1, TILE), w_qkv, w_out, w_up, w_down, cot
+    )
+    layer_out, input_grad, g_qkv, g_out, g_up, g_down = copy_out(
+        [layer_out, input_grad, g_qkv, g_out, g_up, g_down]
+    )
+    block = width // 16
+    mine = lax.dynamic_slice(gains[5], (0, lax.axis_index("dp") * block), (2, block))
+    return (layer_out[None], input_grad[None], mine[1], g_qkv, g_out, mine[0], g_up, g_down)
+
+
+def fits(mesh, tokens, w_qkv, w_up):
+    rows, width, ff = tokens.shape[1] // mesh.shape["blk"], tokens.shape[2], w_up.shape[1]
+    return (
+        mesh.shape["dp"] == 16 and mesh.shape["blk"] == 2 and tokens.shape[0] == 16
+        and rows % TILE == 0 and rows <= 640 and (rows - min(rows, REACH)) % 64 == 0
+        and width == HEADS * 64 and ff == 4 * width
+    )
+
+
 def solution(mesh):
-    return jax.shard_map(
-        per_device,
-        mesh=mesh,
-        in_specs=(
-            P("dp", "blk", None),
-            P("dp", "blk"),
-            P(),
-            P(),
-            P(),
-            P(),
-            P(),
-            P(),
-            P("dp", "blk", None),
-        ),
-        out_specs=(
-            P("dp", "blk", None),
-            P("dp", "blk", None),
-            P("dp"),
-            P("dp", "blk"),
-            P("dp", "blk"),
-            P("dp"),
-            P("dp", "blk"),
-            P("dp", "blk"),
-        ),
-        check_vma=False,
-    )
+    def program(*args):
+        body = fast if fits(mesh, args[0], args[3], args[6]) else per_device
+        rows, whole = P("dp", "blk", None), P()
+        return jax.shard_map(
+            body,
+            mesh=mesh,
+            in_specs=(rows, P("dp", "blk"), whole, whole, whole, whole, whole, whole, rows),
+            out_specs=(rows, rows, P("dp"), P("dp", "blk"), P("dp", "blk"), P("dp"), P("dp", "blk"), P("dp", "blk")),
+            check_vma=False,
+        )(*args)
+
+    return program

time: 1250 us -> 153 us (0.12); the launches traced: 1230 us -> 152 us
  matrix products: 456 us -> 0 us
  local copies, waits for them, and re-layouts: 439 us -> 1.33 us
  Pallas kernels: 0 us -> 150 us
  waiting for transfers between devices: 142 us -> 0 us
  other arithmetic: 109 us -> 0 us
  blocking collectives: 36.1 us -> 0 us
  starting transfers between devices: 31.8 us -> 0 us
  between operations: 15.7 us -> 0.65 us
    dot_general x117 -> x0, matrix products: 456 us -> none  [the longest x30 100 us: block_scores(): jnp.einsum('qhd,khd->hqk', query_rows, keys_rows, preferred_element_type=...]
    dynamic_update_slice x30 -> x0, local copies, waits for them, and re-layouts: 331 us -> none  [attend_backward(): lax.scan(grad_step, start_grad, (keys_blk, vals_blk, seg_blk))]
    pallas_call x0 -> x2, Pallas kernels: none -> 150 us  [the longest x1 146 us: call_layer(): pl.pallas_call(body, out_shape=[jax.ShapeDtypeStruct(v[0], v[1]) for v in...]
    ppermute x6 -> x0, waiting for transfers between devices: 74.3 us -> none  [the longest x2 39.7 us: from_behind(): return lax.ppermute(block, axis, route)]
    reduce_scatter x5 -> x0, waiting for transfers between devices: 50.5 us -> none  [the longest x1 24.6 us: per_device(): lax.psum_scatter(grad_out.astype(jnp.bfloat16), 'dp', scatter_dimension=0...]
    reduce_sum x18 -> x0, other arithmetic: 50 us -> none  [the longest x15 46.4 us: stats_step(): jnp.sum(jnp.where(allowed, jnp.exp(scores - newest[..., None]), 0.0), -1)]
    unnamed x64 -> x0, local copies, waits for them, and re-layouts: 31.3 us -> none
    unnamed x1 -> x0, blocking collectives: 30.6 us -> none
  transfers between devices with their start and end apart: 14 -> 0, of which waited for: 9 -> 0; matrix products, arithmetic and copies ran while one was open for 54% -> 0% of each run, Pallas kernels for 0% -> 0%
where the time goes in v1:
time: 153 us; the launch traced here: 152 us
  Pallas kernels  150 us (98%)
    pallas_call x1, Pallas kernels, call_layer(): pl.pallas_call(body, out_shape=[jax.ShapeDtypeStruct(v[0], v[1]) for v in...  146 us
    pallas_call x1, Pallas kernels, copy_out(): pl.pallas_call(partial(copy_kernel, len(arrays)), out_shape=[jax.ShapeDty...  4.36 us

profile of v1, /device:TPU:0, one launch (start us, length us, event | category | flops | bytes accessed | tf_op | source)
XLA Modules:
  0.0 152.4 jit_solution(479288250625844143)
XLA Ops:
  0.6 146.1 %layer.1 = (f32[640,768]{1,0:T(8,128)}, f32[640,768]{1,0:T(8,128)}, f32[6,8,768]{2,1,0:T(8,128)}, f32[48,1152]{1,0:T(8,128)}, f32[48,384]{1,0:T(8,128)}, /*index=5*/f32[48,1536]{1,0:T(8,128)}, f32[192,384]{1,0:T(8,128)}) custom-call(bf16[640,768]{1,0:T(8,128)(2,1)} %bitcast.10, s32[1,640]{1,0:T(1,128)} %refs_1_.1, f32[6,128]{1,0:T(8,128)} %bitcast.12, ...), custom_call_target="tpu_custom_call" | custom-call | tf_op jit(solution)/shard_map/layer/pallas_call | solution.py:1035
  146.7 4.4 %copy_out.1 = (f32[640,768]{1,0:T(8,128)}, f32[640,768]{1,0:T(8,128)}, f32[48,1152]{1,0:T(8,128)}, f32[48,384]{1,0:T(8,128)}, f32[48,1536]{1,0:T(8,128)}, /*index=5*/f32[192,384]{1,0:T(8,128)}) custom-call(f32[640,768]{1,0:T(8,128)} %get-tuple-element.21.refs_0_, f32[640,768]{1,0:T(8,128)} %get-tuple-element.22.refs_1_, ...), custom_call_target="tpu_custom_call" | custom-call | tf_op jit(solution)/shard_map/copy_out/pallas_call | solution.py:1310
  151.1 0.7 slice.11
  151.8 0.1 constant_dynamic-slice_fusion
  151.9 0.5 slice_bitcast_fusion

commit v2 on v1

--- a/solution.py
+++ b/solution.py
@@ -1289,13 +1289,8 @@
 def copy_kernel(count, *refs):
     source, target, held = refs[:count], refs[count : 2 * count], refs[2 * count : 3 * count]
     sems = refs[3 * count]
-    pieces = []
-    for k in range(count):
-        rows = source[k].shape[0]
-        step = rows // 4 if rows % 64 == 0 else rows
-        pieces += [(k, pl.ds(at, step)) for at in range(0, rows, step)]
-    loads = [pltpu.make_async_copy(source[k].at[at], held[k].at[at], sems.at[0, n]) for n, (k, at) in enumerate(pieces)]
-    stores = [pltpu.make_async_copy(held[k].at[at], target[k].at[at], sems.at[1, n]) for n, (k, at) in enumerate(pieces)]
+    loads = [pltpu.make_async_copy(source[k], held[k], sems.at[0, k]) for k in range(count)]
+    stores = [pltpu.make_async_copy(held[k], target[k], sems.at[1, k]) for k in range(count)]
     for copy in loads:
         copy.start()
     for load, store in zip(loads, stores):
@@ -1313,7 +1308,7 @@
         in_specs=[anywhere] * len(arrays),
         out_specs=[anywhere] * len(arrays),
         scratch_shapes=[pltpu.VMEM(a.shape, a.dtype) for a in arrays]
-        + [pltpu.SemaphoreType.DMA((2, 4 * len(arrays)))],
+        + [pltpu.SemaphoreType.DMA((2, len(arrays)))],
         name="copy_out",
     )(*arrays)
 

time: 153 us -> 152 us (level)
  no operation moved by 1% of the time
where the time goes in v2:
time: 152 us
  Pallas kernels  150 us (99%)
    pallas_call x1, Pallas kernels, call_layer(): pl.pallas_call(body, out_shape=[jax.ShapeDtypeStruct(v[0], v[1]) for v in...  146 us
    pallas_call x1, Pallas kernels, copy_out(): pl.pallas_call(partial(copy_kernel, len(arrays)), out_shape=[jax.ShapeDty...  3.85 us

profile of v2, /device:TPU:0, one launch (start us, length us, event | category | flops | bytes accessed | tf_op | source)
XLA Modules:
  0.0 151.9 jit_solution(10742151872029297379)
XLA Ops:
  0.6 146.1 %layer.1 = (f32[640,768]{1,0:T(8,128)}, f32[640,768]{1,0:T(8,128)}, f32[6,8,768]{2,1,0:T(8,128)}, f32[48,1152]{1,0:T(8,128)}, f32[48,384]{1,0:T(8,128)}, /*index=5*/f32[48,1536]{1,0:T(8,128)}, f32[192,384]{1,0:T(8,128)}) custom-call(bf16[640,768]{1,0:T(8,128)(2,1)} %bitcast.10, s32[1,640]{1,0:T(1,128)} %refs_1_.1, f32[6,128]{1,0:T(8,128)} %bitcast.12, ...), custom_call_target="tpu_custom_call" | custom-call | tf_op jit(solution)/shard_map/layer/pallas_call | solution.py:1035
  146.7 3.8 %copy_out.1 = (f32[640,768]{1,0:T(8,128)}, f32[640,768]{1,0:T(8,128)}, f32[48,1152]{1,0:T(8,128)}, f32[48,384]{1,0:T(8,128)}, f32[48,1536]{1,0:T(8,128)}, /*index=5*/f32[192,384]{1,0:T(8,128)}) custom-call(f32[640,768]{1,0:T(8,128)} %get-tuple-element.21.refs_0_, f32[640,768]{1,0:T(8,128)} %get-tuple-element.22.refs_1_, ...), custom_call_target="tpu_custom_call" | custom-call | tf_op jit(solution)/shard_map/copy_out/pallas_call | solution.py:1305
  150.6 0.7 slice.11
  151.3 0.1 constant_dynamic-slice_fusion
  151.4 0.5 slice_bitcast_fusion
